TPU v7x, 32 devices: a whole 2x2x4 slice. The times are simulated.
32 devices in a mesh: grp: 2 (over y), rows: 8 (over z, x), cols: 2 (over core).
Axes of the slice: x: 2, y: 2, z: 4, core: 2. Of those that a mesh axis runs over, the one named last changes fastest.
Arguments:
- masks: bfloat16 [2560, 25088], P(('grp', 'rows'), 'cols'), parts along dimension 0, may hold values from 0 to 1, as said below
- targets: float32 [2, 2560, 40], P(None, ('grp', 'rows')), parts along dimension 1, may hold values from -6 to 6
- weights_in: float32 [80, 25088], P('grp', ('cols', 'rows')), parts along dimension 0, may hold values from -5 to 5
- bias_in: float32 [80], P('grp'), parts along dimension 0, may hold values from -5 to 5
- threshold: float32 [80], P('grp'), parts along dimension 0, may hold values from 0.05 to 0.4
- live_pairs: int32 [16], P(('grp', 'rows')), parts along dimension 0, may hold values from 40 to 160, as said below
Outputs:
- weights: float32 [80, 25088], P('grp', ('cols', 'rows')), parts along dimension 0
- bias: float32 [80], P('grp'), parts along dimension 0
- residual: float32 [2, 2560, 40], P(None, ('grp', 'rows')), parts along dimension 1
There are 2 independent parts, one for each index of `grp`. A program takes and returns all parts, laid end to end along the dimension named above; each array names one. Nothing has to cross between parts.
Inputs may be any that keep to these rules, and one draw needn't show every extreme that they name: `masks`: each entry is 0 or 1. `live_pairs`: A device's live pairs are its first slots; in every draw some device has all 160 slots live.
All inputs are finite; a program needn't handle non-finite values.
Results may differ from a plain program's by a relative error of at most 0.0052.
Values may be sent and summed in bfloat16 or wider, within the bound.
A program may use at most 64 MiB of HBM per device.

v0:
```python
import math

import jax
import jax.numpy as jnp
from jax import lax
from jax.sharding import PartitionSpec as P

N = 25088
ITERS = 2


def shrink(values, threshold):
    bound = threshold[:, None]
    return values - jnp.clip(values, -bound, bound)


def on_device(masks, targets, weights_in, bias_in, threshold, live_pairs):
    slots = masks.shape[0]
    scale = 1.0 / math.sqrt(N)
    live = (lax.broadcasted_iota(jnp.int32, (slots, 1), 0) < live_pairs[0]).astype(jnp.float32)
    count = 2.0 * lax.psum(live_pairs[0].astype(jnp.float32), "rows")
    factor = 0.2 * N * scale / count
    signed = masks * 2 - 1
    along_rows = (((1,), (1,)), ((), ()))
    along_slots = (((0,), (0,)), ((), ()))
    doubled = jnp.concatenate([signed, -signed], 0)
    bias = bias_in
    upper = None
    lower = None
    whole = lax.all_gather(weights_in, "rows", axis=1, tiled=True)
    for iteration in range(ITERS + 1):
        partial_scores = lax.dot_general(
            doubled, whole.astype(jnp.bfloat16), along_rows, preferred_element_type=jnp.float32
        )
        total = lax.psum(partial_scores, "cols") * scale
        first = total[:slots]
        second = total[slots:]
        residuals_upper = live * (first + bias - targets[0])
        residuals_lower = live * (second + bias - targets[1])
        upper = residuals_upper
        lower = residuals_lower
        if iteration < ITERS:
            upper16 = upper.astype(jnp.bfloat16)
            lower16 = lower.astype(jnp.bfloat16)
            stacked = jnp.concatenate([upper16, lower16], 0)
            gradient_part = lax.dot_general(
                stacked, doubled, along_slots, preferred_element_type=jnp.float32
            )
            gradient_part, bias_part = (gradient_part, jnp.sum(upper + lower, 0))
            gradient_sum, bias_sum = lax.psum((gradient_part, bias_part), "rows")
            whole = shrink(whole - factor * gradient_sum, threshold)
            bias = bias - 0.5 * bias_sum / count
    share = weights_in.shape[1]
    weights = lax.dynamic_slice_in_dim(whole, lax.axis_index("rows") * share, share, 1)
    residual = jnp.stack([upper, lower], 0)
    return (weights, bias, residual)


def solution(mesh):
    return jax.shard_map(
        on_device,
        mesh=mesh,
        in_specs=(
            P(("grp", "rows"), "cols"),
            P(None, ("grp", "rows"), None),
            P("grp", ("cols", "rows")),
            P("grp"),
            P("grp"),
            P(("grp", "rows")),
        ),
        out_specs=(P("grp", ("cols", "rows")), P("grp"), P(None, ("grp", "rows"), None)),
        check_vma=False,
    )
```

profile of v0, /device:TPU:1, one launch (start us, length us, event | category | flops | bytes accessed | tf_op | source)
XLA Modules:
  0.0 315.8 jit_solution(12114016251493410935)
XLA Ops:
  7.2 0.0 all-gather.3.cloned.1.call-start
  7.2 0.7 all-gather.3.cloned.1.call-update
  7.9 0.0 all-reduce.4.cloned.1.call-start
  8.6 5.9 %multiply_add_fusion = (bf16[160,12544]{1,0:T(8,128)(2,1)}, bf16[160,12544]{1,0:T(8,128)(2,1)}) fusion(bf16[160,12544]{1,0:T(8,128)(2,1)} %param.6), kind=kLoop, calls=%fused_computation.1 | loop fusion | flops 6021120 | bytes 12042240 | tf_op jit(solution)/shard_map/sub | solution.py:23
  14.5 46.5 %all-gather.3.cloned.1.call-done = f32[8,1568,40]{1,2,0:T(8,128)} async-done(((f32[1,1568,40]{1,2,0:T(8,128)}), f32[8,1568,40]{1,2,0:T(8,128)}) %all-gather.3.cloned.1.call-update) | async-done | bytes 2007056 | tf_op jit(solution)/shard_map/all_gather | solution.py:30
  61.0 2.0 copy.10
  63.0 1.9 reshape.20
  64.9 6.3 %fusion = f32[320,40]{0,1:T(8,128)S(1)} fusion(bf16[160,12544]{1,0:T(8,128)(2,1)} %get-tuple-element.6, bf16[160,12544]{1,0:T(8,128)(2,1)} %get-tuple-element.5, f32[12544,40]{0,1:T(8,128)} %reshape.20), kind=kOutput, calls=%fused_computation.6 | convolution fusion | flops 337182720 | bytes 10086400 | tf_op jit(solution)/shard_map/dot_general | solution.py:32
  71.3 5.2 %psum.57 = f32[320,40]{0,1:T(8,128)S(1)} all-reduce(f32[320,40]{0,1:T(8,128)S(1)} %fusion), channel_id=1, replica_groups=mesh['grp'=2,'rows'=8,'cols'=2] {'cols'}, use_global_device_ids=true, to_apply=%region_1.0 | all-reduce | flops 12800 | bytes 102400 | tf_op jit(solution)/shard_map/psum | solution.py:35
  76.5 0.2 fusion.29
  76.7 6.2 %fusion.19 = f32[40,12544]{1,0:T(8,128)} fusion(bf16[160,40]{0,1:T(8,128)(2,1)S(1)} %get-tuple-element.14, bf16[160,40]{0,1:T(8,128)(2,1)S(1)} %get-tuple-element.12, bf16[160,12544]{1,0:T(8,128)(2,1)} %get-tuple-element.6, bf16[160,12544]{1,0:T(8,128)(2,1)} %get-tuple-element.5), kind=kOutput, calls=%fused_computation.34 | convolution fusion | flops 337233920 | bytes 10060800 | tf_op jit(solution)/shard_map/dot_general | solution.py:46
  82.9 0.0 all-reduce.4.cloned.1.call-update
  82.9 0.0 all-reduce.6.cloned.1.call-start
  83.0 0.0 copy-done.6
  83.0 16.2 %all-reduce = (f32[40]{0:T(128)S(1)}, f32[]{:T(128)}) all-reduce(f32[40]{0:T(128)S(1)} %get-tuple-element.13, f32[]{:T(128)S(6)} %convert_element_type.32), channel_id=1, replica_groups=mesh['grp'=2,'rows'=8,'cols'=2] {'rows'}, use_global_device_ids=true, to_apply=%region_5.6 | all-reduce | flops 41 | bytes 328 | tf_op jit(solution)/shard_map/psum | solution.py:50
  99.9 80.7 %all-reduce.4.cloned.1.call-done = f32[40,12544]{1,0:T(8,128)} async-done(((f32[40,12544]{1,0:T(8,128)}), f32[40,12544]{1,0:T(8,128)}) %all-reduce.4.cloned.1.call-update) | async-done | bytes 2007056 | tf_op jit(solution)/shard_map/psum | solution.py:50
  180.6 0.0 copy-done
  180.6 6.3 %fusion.3 = f32[320,40]{0,1:T(8,128)S(1)} fusion(f32[12544,40]{0,1:T(8,128)S(1)} %copy-done, f32[40,12544]{1,0:T(8,128)} %all-reduce.4.cloned.1.call-done, f32[40]{0:T(128)S(1)} %neg.9, f32[40]{0:T(128)S(1)} %copy-done.6, f32[]{:T(128)S(6)} %div.13, bf16[160,12544]{1,0:T(8,128)(2,1)} %get-tuple-element.6, bf16[160,12544]{1,0:T(8,128)(2,1)} %get-tuple-element.5), kind=kOutput, calls=%fused_computation.9 | convolution fusion | flops 340193280 | bytes 12093764 | tf_op jit(solution)/shard_map/dot_general | solution.py:32
  187.0 4.3 %psum.59 = f32[320,40]{0,1:T(8,128)S(1)} all-reduce(f32[320,40]{0,1:T(8,128)S(1)} %fusion.3), channel_id=1, replica_groups=mesh['grp'=2,'rows'=8,'cols'=2] {'cols'}, use_global_device_ids=true, to_apply=%region_3.0 | all-reduce | flops 12800 | bytes 102400 | tf_op jit(solution)/shard_map/psum | solution.py:35
  191.3 0.2 add_reduce_fusion
  191.5 6.1 %fusion.23 = f32[40,12544]{1,0:T(8,128)} fusion(bf16[160,40]{0,1:T(8,128)(2,1)S(1)} %get-tuple-element.11, bf16[160,40]{0,1:T(8,128)(2,1)S(1)} %get-tuple-element.10, bf16[160,12544]{1,0:T(8,128)(2,1)} %get-tuple-element.6, bf16[160,12544]{1,0:T(8,128)(2,1)} %get-tuple-element.5), kind=kOutput, calls=%fused_computation.38 | convolution fusion | flops 337233920 | bytes 10060800 | tf_op jit(solution)/shard_map/dot_general | solution.py:46
  197.5 0.0 all-reduce.6.cloned.1.call-update
  197.5 16.8 %psum.62 = f32[40]{0:T(128)S(1)} all-reduce(f32[40]{0:T(128)S(1)} %get-tuple-element.9), channel_id=1, replica_groups=mesh['grp'=2,'rows'=8,'cols'=2] {'rows'}, use_global_device_ids=true, to_apply=%region_8.9 | all-reduce | flops 40 | bytes 320 | tf_op jit(solution)/shard_map/psum | solution.py:50
  214.4 82.1 %all-reduce.6.cloned.1.call-done = f32[40,12544]{1,0:T(8,128)} async-done(((f32[40,12544]{1,0:T(8,128)}), f32[40,12544]{1,0:T(8,128)}) %all-reduce.6.cloned.1.call-update) | async-done | bytes 2007056 | tf_op jit(solution)/shard_map/psum | solution.py:50
  296.5 3.0 minimum_subtract_fusion
  299.5 0.3 copy-done.1
  299.8 1.2 copy-done.2
  301.0 2.4 fusion.1
  303.4 0.8 constant_dynamic-slice_fusion
  304.3 4.3 %psum.63 = f32[320,40]{0,1:T(8,128)S(1)} all-reduce(f32[320,40]{0,1:T(8,128)S(1)} %fusion.1), channel_id=1, replica_groups=mesh['grp'=2,'rows'=8,'cols'=2] {'cols'}, use_global_device_ids=true, to_apply=%region_9.10 | all-reduce | flops 12800 | bytes 102400 | tf_op jit(solution)/shard_map/psum | solution.py:35
  308.6 0.1 fusion.10
  308.7 0.6 pad_maximum_fusion.1
  (17 shorter events, 0.1 us)
Async XLA Ops:
  7.2 53.8 %all-gather.3.cloned.1.call-start = ((), (), s32[]{:S(2)}) async-start(), calls=%async_computation.2 | async-start | bytes 2396160 | tf_op jit(solution)/shard_map/all_gather | solution.py:30
  7.9 172.7 %all-reduce.4.cloned.1.call-start = ((), (), s32[]{:S(2)}) async-start(), calls=%async_computation | async-start | bytes 4014080 | tf_op jit(solution)/shard_map/psum | solution.py:50
  64.9 11.6 %copy-start.3 = (f32[2,160,40]{1,2,0:T(8,128)S(1)}, f32[2,160,40]{1,2,0:T(8,128)}, u32[]{:S(2)}) copy-start(f32[2,160,40]{1,2,0:T(8,128)} %param.7) | copy-start | bytes 153604
  64.9 11.6 %copy-start.4 = (f32[40]{0:T(128)S(1)}, f32[40]{0:T(128)}, u32[]{:S(2)}) copy-start(f32[40]{0:T(128)} %param.9) | copy-start | bytes 484
  76.7 6.3 %copy-start.6 = (f32[40]{0:T(128)S(1)}, f32[40]{0:T(128)}, u32[]{:S(2)}) copy-start(f32[40]{0:T(128)} %param.10) | copy-start | bytes 484
  76.7 103.9 %copy-start = (f32[12544,40]{0,1:T(8,128)S(1)}, f32[12544,40]{0,1:T(8,128)}, u32[]{:S(2)}) copy-start(f32[12544,40]{0,1:T(8,128)} %reshape.20) | copy-start | bytes 6021124
  82.9 213.5 %all-reduce.6.cloned.1.call-start = ((), (), s32[]{:S(2)}) async-start(), calls=%async_computation.1 | async-start | bytes 4014080 | tf_op jit(solution)/shard_map/psum | solution.py:50
  214.4 94.2 %copy-start.5 = (f32[40]{0:T(128)}, f32[40]{0:T(128)S(1)}, u32[]{:S(2)}) copy-start(f32[40]{0:T(128)S(1)} %divide_subtract_fusion) | copy-start | bytes 484
  296.5 3.3 %copy-start.1 = (bf16[160,12544]{1,0:T(8,128)(2,1)S(1)}, bf16[160,12544]{1,0:T(8,128)(2,1)}, u32[]{:S(2)}) copy-start(bf16[160,12544]{1,0:T(8,128)(2,1)} %get-tuple-element.5) | copy-start | bytes 12042244
  296.5 4.6 %copy-start.2 = (bf16[160,12544]{1,0:T(8,128)(2,1)S(1)}, bf16[160,12544]{1,0:T(8,128)(2,1)}, u32[]{:S(2)}) copy-start(bf16[160,12544]{1,0:T(8,128)(2,1)} %get-tuple-element.6) | copy-start | bytes 12042244
Sparse Core Ops, SparseCore 0:
  10.2 50.7 all-gather.2
  83.0 97.5 all-reduce.3
  197.7 98.7 all-reduce.5
where the time goes:
time: 316 us
  waiting for transfers between devices  210 us (66%)
  blocking collectives  46.7 us (15%)
  matrix products  27.3 us (9%)
  between operations  15.2 us (5%)
  other arithmetic  10 us (3%)
  local copies, waits for them, and re-layouts  6.37 us (2%)
    psum x2, waiting for transfers between devices, on_device(): gradient_sum, bias_sum = lax.psum((gradient_part, bias_part), 'rows')  163 us
    all_gather x1, waiting for transfers between devices, on_device(): whole = lax.all_gather(weights_in, 'rows', axis=1, tiled=True)  46.5 us
    psum x2, blocking collectives, on_device(): gradient_sum, bias_sum = lax.psum((gradient_part, bias_part), 'rows')  33 us
    dot_general x3, matrix products, on_device(): lax.dot_general(doubled, whole.astype(jnp.bfloat16), along_rows, preferre...  15.1 us
    psum x3, blocking collectives, on_device(): total = lax.psum(partial_scores, 'cols') * scale  13.7 us
    dot_general x2, matrix products, on_device(): lax.dot_general(stacked, doubled, along_slots, preferred_element_type=jnp...  12.2 us
  transfers between devices with their start and end apart: 3, of which 3 were waited for; matrix products, arithmetic and copies ran while one was open for 2% of the time, Pallas kernels for 0%

commit v1 on v0

v1 whole, which is shorter than its diff:
```python
import functools
import math

import jax
import jax.numpy as jnp
from jax import lax
from jax.experimental import pallas as pl
from jax.experimental.pallas import tpu as pltpu
from jax.sharding import PartitionSpec as P

N = 25088
ITERS = 2
LANES = 128
F32 = jnp.float32
BF16 = jnp.bfloat16


def shrink(values, bound):
    return values - jnp.clip(values, -bound, bound)


def plain(masks, targets, weights_in, bias_in, threshold, live_pairs):
    slots = masks.shape[0]
    scale = 1.0 / math.sqrt(N)
    live = (lax.broadcasted_iota(jnp.int32, (slots, 1), 0) < live_pairs[0]).astype(F32)
    count = 2.0 * lax.psum(live_pairs[0].astype(F32), "rows")
    factor = 0.2 * N * scale / count
    signed = masks * 2 - 1
    bias = bias_in
    share = weights_in.shape[1]
    whole = lax.all_gather(weights_in, "rows", axis=1, tiled=True)
    for iteration in range(ITERS + 1):
        part = lax.dot_general(
            signed, whole.astype(BF16), (((1,), (1,)), ((), ())), preferred_element_type=F32
        )
        total = lax.psum(part, "cols") * scale
        upper = live * (total + bias - targets[0])
        lower = live * (-total + bias - targets[1])
        if iteration < ITERS:
            stacked = jnp.concatenate([upper.astype(BF16), lower.astype(BF16)], 1)
            both = lax.dot_general(
                stacked, signed, (((0,), (0,)), ((), ())), preferred_element_type=F32
            )
            k = upper.shape[1]
            raw, bias_sum = lax.psum((both[:k] - both[k:], jnp.sum(upper + lower, 0)), "rows")
            whole = shrink(whole - factor * raw, threshold[:, None])
            bias = bias - 0.5 * bias_sum / count
    weights = lax.dynamic_slice_in_dim(whole, lax.axis_index("rows") * share, share, 1)
    return weights, bias, jnp.stack([upper, lower], 0)


def body(
    tiles, nz,
    masks_hbm, targets, w_in, bias_in, thr, live_pairs,
    w_out, b_out, res_out,
    sm, wf, ag, xs, xr, zs, zr, bs, br, ss, sr,
    mask_sem, own_send, fwd_send, z_recv, x_recv,
    xs_send, xs_recv, zs_send, zs_recv, b_send, b_recv, s_send, s_recv,
):
    k_rows, share = w_in.shape
    slots = sm.shape[0]
    win = tiles * LANES
    half = (tiles + 1) // 2 * LANES
    tail = win - half
    scale = 1.0 / math.sqrt(N)

    r = lax.axis_index("rows")
    c = lax.axis_index("cols")
    z = r // 2
    x = r % 2
    xpeer = z * 2 + (1 - x)

    def owner(k, other):
        zk = lax.rem(z + k, nz)
        return zk * 2 + ((1 - x) if other else x)

    def sender_to(k, other):
        zk = lax.rem(z + (nz - k), nz)
        return zk * 2 + ((1 - x) if other else x)

    def start_of(o):
        return pl.multiple_of((o * share) // LANES * LANES, LANES)

    offset = r * share - (r * share) // LANES * LANES

    mask_copy = pltpu.make_async_copy(masks_hbm, sm, mask_sem)
    mask_copy.start()

    barrier = pltpu.get_barrier_semaphore()
    for k in range(nz):
        for other in (0, 1):
            if k or other:
                pl.semaphore_signal(
                    barrier, inc=1, device_id={"rows": owner(k, other)},
                    device_id_type=pl.DeviceIdType.MESH,
                )
    pl.semaphore_signal(
        barrier, inc=1, device_id={"cols": 1 - c}, device_id_type=pl.DeviceIdType.MESH
    )

    pending = []

    def send(src, dst, ssem, rsem, where):
        copy = pltpu.make_async_remote_copy(
            src_ref=src, dst_ref=dst, send_sem=ssem, recv_sem=rsem,
            device_id=where, device_id_type=pl.DeviceIdType.MESH,
        )
        copy.start()
        pending.append(copy)
        return copy

    def pack(value, ref):
        ref[:, 0:win] = value[0:16].astype(BF16)
        ref[:, win : 2 * win] = value[16:32].astype(BF16)
        last = value[32:40]
        ref[:, 2 * win : 2 * win + half] = jnp.concatenate(
            [last[:, :half], last[:, win - half :]], 0
        ).astype(BF16)

    def unpack(ref):
        both = ref[:, 2 * win : 2 * win + half].astype(F32)
        last = jnp.concatenate([both[:8], both[8:, half - tail :]], 1)
        return jnp.concatenate(
            [ref[:, 0:win].astype(F32), ref[:, win : 2 * win].astype(F32), last], 0
        )

    lane = lax.broadcasted_iota(jnp.int32, (1, win), 1)
    mine = (lane >= offset) & (lane < offset + share)
    wf[:, 0:share] = w_in[...]
    wf[:, share:win] = jnp.zeros((k_rows, win - share), F32)
    wf[...] = pltpu.roll(wf[...], offset, 1)
    pack(wf[...], ag.at[0, 0, 0])

    pl.semaphore_wait(barrier, 2 * nz)

    def send_own(t):
        own = ag.at[t, 0, 0]
        send(own, ag.at[t, 0, 1], own_send.at[t, 0], x_recv.at[t, 0], {"rows": xpeer})
        for k in range(1, nz):
            send(own, ag.at[t, k, 0], own_send.at[t, k], z_recv.at[t, k], {"rows": sender_to(k, 0)})

    def window_scores(t, k, other):
        block = unpack(ag.at[t, k, other]).astype(BF16)
        start = start_of(owner(k, other))
        return lax.dot_general(
            block, sm[:, pl.ds(start, win)], (((1,), (1,)), ((), ())), preferred_element_type=F32
        )

    def recv(dst, rsem):
        pltpu.make_async_copy(dst, dst, rsem).wait()

    send_own(0)
    mask_copy.wait()
    for i in range(slots // 16):
        rows = pl.ds(i * 16, 16)
        sm[rows, :] = sm[rows, :] * 2 - 1

    live = (lax.broadcasted_iota(jnp.int32, (1, slots), 1) < live_pairs[0]).astype(F32)
    eye = (
        lax.broadcasted_iota(jnp.int32, (k_rows, LANES), 0)
        == lax.broadcasted_iota(jnp.int32, (k_rows, LANES), 1)
    ).astype(F32)
    last_lane = lax.broadcasted_iota(jnp.int32, (1, LANES), 1) == LANES - 1
    bias = bias_in[...]
    bound = thr[...]

    def gradient(stacked, k, other):
        start = start_of(owner(k, other))
        both = jnp.dot(stacked, sm[:, pl.ds(start, win)], preferred_element_type=F32)
        return both[:k_rows] - both[k_rows:]

    for t in range(ITERS + 1):
        part = window_scores(t, 0, 0)
        for k in range(1, nz):
            recv(ag.at[t, k, 0], z_recv.at[t, k])
            send(ag.at[t, k, 0], ag.at[t, k, 1], fwd_send.at[t, k], x_recv.at[t, k], {"rows": xpeer})
            part += window_scores(t, k, 0)
        for k in range(nz):
            recv(ag.at[t, k, 1], x_recv.at[t, k])
            part += window_scores(t, k, 1)

        ss[t] = part
        copy = send(ss.at[t], sr.at[t], s_send.at[t], s_recv.at[t], {"cols": 1 - c})
        copy.wait_recv()
        total = (part + sr[t]) * scale
        upper = live * (total + bias - targets[0])
        lower = live * (-total + bias - targets[1])
        if t == ITERS:
            res_out[0] = upper
            res_out[1] = lower
            break

        stacked = jnp.concatenate([upper, lower], 0).astype(BF16)
        order = list(range(1, nz)) + [0]
        for k in order:
            pack(gradient(stacked, k, 1), xs.at[t, k])
            send(xs.at[t, k], xr.at[t, k], xs_send.at[t, k], xs_recv.at[t, k], {"rows": xpeer})

        column = jnp.sum(upper + lower, 1, keepdims=True)
        row = jnp.sum(column * eye, 0, keepdims=True)
        row = jnp.where(last_lane, live_pairs[0].astype(F32), row)
        bs[t] = jnp.broadcast_to(row, (8, LANES))
        br[t, r] = jnp.broadcast_to(row, (8, LANES))
        for k in range(nz):
            for other in (0, 1):
                if k or other:
                    send(
                        bs.at[t], br.at[t, r], b_send.at[t, k, other], b_recv.at[t, k, other],
                        {"rows": sender_to(k, other)},
                    )

        for k in range(1, nz):
            own = gradient(stacked, k, 0)
            recv(xr.at[t, k], xs_recv.at[t, k])
            pack(own + unpack(xr.at[t, k]), zs.at[t, k])
            send(zs.at[t, k], zr.at[t, k], zs_send.at[t, k], zs_recv.at[t, k], {"rows": owner(k, 0)})
        raw = gradient(stacked, 0, 0)
        recv(xr.at[t, 0], xs_recv.at[t, 0])
        raw += unpack(xr.at[t, 0])

        for k in range(nz):
            for other in (0, 1):
                if k or other:
                    recv(br.at[t, owner(k, other)], b_recv.at[t, k, other])
        sums = br[t, 0]
        for j in range(1, 2 * nz):
            sums += br[t, j]
        sums = sums[0:1]
        count = 2.0 * jnp.sum(jnp.where(last_lane, sums, 0.0), 1, keepdims=True)
        bias_sum = jnp.sum(sums * eye, 1, keepdims=True)
        factor = 0.2 * N * scale / count
        bias = bias - 0.5 * bias_sum / count

        for k in range(1, nz):
            recv(zr.at[t, k], zs_recv.at[t, k])
            raw += unpack(zr.at[t, k])
        new = jnp.where(mine, shrink(wf[...] - factor * raw, bound), 0.0)
        wf[...] = new
        pack(new, ag.at[t + 1, 0, 0])
        send_own(t + 1)

    b_out[...] = bias
    w_out[...] = pltpu.roll(wf[...], lax.rem(win - offset, win), 1)[:, :share]
    for copy in pending:
        copy.wait_send()


def fused(rows, masks, targets, weights_in, bias_in, threshold, live_pairs):
    slots, cols = masks.shape
    k_rows, share = weights_in.shape
    nz = rows // 2
    tiles = max(-(-share * (j + 1) // LANES) - share * j // LANES for j in range(rows))
    packed = (16, 2 * tiles * LANES + (tiles + 1) // 2 * LANES)
    turns = ITERS + 1
    dma = pltpu.SemaphoreType.DMA
    vmem = pl.BlockSpec(memory_space=pltpu.VMEM)
    weights, bias, residual = pl.pallas_call(
        functools.partial(body, tiles, nz),
        out_shape=(
            jax.ShapeDtypeStruct((k_rows, share), F32),
            jax.ShapeDtypeStruct((k_rows, 1), F32),
            jax.ShapeDtypeStruct((2, k_rows, slots), F32),
        ),
        in_specs=[
            pl.BlockSpec(memory_space=pl.ANY), vmem, vmem, vmem, vmem,
            pl.BlockSpec(memory_space=pltpu.SMEM),
        ],
        out_specs=(vmem, vmem, vmem),
        scratch_shapes=[
            pltpu.VMEM((slots, cols), BF16),
            pltpu.VMEM((k_rows, tiles * LANES), F32),
            pltpu.VMEM((turns, nz, 2) + packed, BF16),
            pltpu.VMEM((ITERS, nz) + packed, BF16),
            pltpu.VMEM((ITERS, nz) + packed, BF16),
            pltpu.VMEM((ITERS, nz) + packed, BF16),
            pltpu.VMEM((ITERS, nz) + packed, BF16),
            pltpu.VMEM((ITERS, 8, LANES), F32),
            pltpu.VMEM((ITERS, rows, 8, LANES), F32),
            pltpu.VMEM((turns, k_rows, slots), F32),
            pltpu.VMEM((turns, k_rows, slots), F32),
            dma,
            dma((turns, nz)), dma((turns, nz)), dma((turns, nz)), dma((turns, nz)),
            dma((ITERS, nz)), dma((ITERS, nz)), dma((ITERS, nz)), dma((ITERS, nz)),
            dma((ITERS, nz, 2)), dma((ITERS, nz, 2)),
            dma((turns,)), dma((turns,)),
        ],
        compiler_params=pltpu.CompilerParams(
            collective_id=0, has_side_effects=True, vmem_limit_bytes=48 * 1024 * 1024
        ),
    )(
        masks, jnp.swapaxes(targets, 1, 2), weights_in,
        bias_in[:, None], threshold[:, None], live_pairs,
    )
    return weights, bias[:, 0], jnp.swapaxes(residual, 1, 2)


def solution(mesh):
    rows = mesh.shape["rows"]
    on_device = functools.partial(fused, rows) if rows == 8 else plain
    return jax.shard_map(
        on_device,
        mesh=mesh,
        in_specs=(
            P(("grp", "rows"), "cols"),
            P(None, ("grp", "rows"), None),
            P("grp", ("cols", "rows")),
            P("grp"),
            P("grp"),
            P(("grp", "rows")),
        ),
        out_specs=(P("grp", ("cols", "rows")), P("grp"), P(None, ("grp", "rows"), None)),
        check_vma=False,
    )
```

time: 316 us -> 114 us (0.36)
  waiting for transfers between devices: 210 us -> 0 us
  Pallas kernels: 0 us -> 105 us
  blocking collectives: 46.7 us -> 0 us
  matrix products: 27.3 us -> 0 us
  between operations: 15.2 us -> 1.29 us
  other arithmetic: 10 us -> 0.63 us
    psum x2 -> x0, waiting for transfers between devices: 163 us -> none  [on_device(): gradient_sum, bias_sum = lax.psum((gradient_part, bias_part), 'rows')]
    pallas_call x0 -> x1, Pallas kernels: none -> 105 us  [fused(): pl.pallas_call(functools.partial(body, tiles, nz), out_shape=(jax.ShapeDt...]
    psum x5 -> x0, blocking collectives: 46.7 us -> none  [the longest x2 33 us: on_device(): gradient_sum, bias_sum = lax.psum((gradient_part, bias_part), 'rows')]
    all_gather x1 -> x0, waiting for transfers between devices: 46.5 us -> none  [on_device(): whole = lax.all_gather(weights_in, 'rows', axis=1, tiled=True)]
    dot_general x5 -> x0, matrix products: 27.3 us -> none  [the longest x3 15.1 us: on_device(): lax.dot_general(doubled, whole.astype(jnp.bfloat16), along_rows, preferre...]
    sub x4 -> x0, other arithmetic: 8.88 us -> none  [the longest x1 5.86 us: on_device(): signed = masks * 2 - 1]
  transfers between devices with their start and end apart: 3 -> 0, of which waited for: 3 -> 0; matrix products, arithmetic and copies ran while one was open for 2% -> 0% of each run, Pallas kernels for 0% -> 0%
where the time goes in v1:
time: 114 us
  Pallas kernels  105 us (92%)
  local copies, waits for them, and re-layouts  6.79 us (6%)
  between operations  1.29 us (1%)
    pallas_call x1, Pallas kernels, fused(): pl.pallas_call(functools.partial(body, tiles, nz), out_shape=(jax.ShapeDt...  105 us
    unnamed x8, local copies, waits for them, and re-layouts  5.31 us

profile of v1, /device:TPU:1, one launch (start us, length us, event | category | flops | bytes accessed | tf_op | source)
XLA Modules:
  0.0 113.9 jit_solution(4409911465317683132)
XLA Ops:
  1.3 0.7 copy.11.bias_in
  2.0 0.7 copy.12.thr
  2.8 0.0 copy-start
  2.8 2.1 %copy-done = bf16[160,12544]{1,0:T(8,128)(2,1)S(1)} copy-done((bf16[160,12544]{1,0:T(8,128)(2,1)S(1)}, bf16[160,12544]{1,0:T(8,128)(2,1)}, u32[]{:S(2)}) %copy-start) | copy-done | bytes 4014104
  4.9 0.0 copy-start.1
  4.9 0.9 copy-done.1
  5.8 0.0 copy-start.2
  5.8 0.9 copy-done.2
  6.7 105.1 %shard_map.85 = (f32[40,1568]{1,0:T(8,128)S(1)}, f32[40,1]{1,0:T(8,128)S(1)}, f32[2,40,160]{2,1,0:T(8,128)S(1)}) custom-call(bf16[160,12544]{1,0:T(8,128)(2,1)S(1)} %copy-done, f32[2,40,160]{2,1,0:T(8,128)S(1)} %bitcast.5, f32[40,1568]{1,0:T(8,128)S(1)} %copy-done.1, f32[40,1]{1,0:T(8,128)S(1)} %copy.11.bias_in, f32[40,1]{1,0:T(8,128)S(1)} %copy.12.thr, ...), custom_call_target="tpu_custom_call" | custom-call | tf_op jit(solution)/shard_map/pallas_call | solution.py:257
  111.9 0.6 reduce
  112.5 0.7 copy.16
  113.2 0.6 copy.17
Async XLA Ops:
  2.8 2.1 %copy-start = (bf16[160,12544]{1,0:T(8,128)(2,1)S(1)}, bf16[160,12544]{1,0:T(8,128)(2,1)}, u32[]{:S(2)}) copy-start(bf16[160,12544]{1,0:T(8,128)(2,1)} %masks_hbm.1) | copy-start | bytes 12042244
  4.9 1.0 copy-start.1
  5.8 0.9 copy-start.2

commit v2 on v1

v2 whole, which is shorter than its diff:
```python
import functools
import math

import jax
import jax.numpy as jnp
from jax import lax
from jax.experimental import pallas as pl
from jax.experimental.pallas import tpu as pltpu
from jax.sharding import PartitionSpec as P

N = 25088
ITERS = 2
LANES = 128
F32 = jnp.float32
BF16 = jnp.bfloat16


def shrink(values, bound):
    return values - jnp.clip(values, -bound, bound)


def plain(masks, targets, weights_in, bias_in, threshold, live_pairs):
    slots = masks.shape[0]
    scale = 1.0 / math.sqrt(N)
    live = (lax.broadcasted_iota(jnp.int32, (slots, 1), 0) < live_pairs[0]).astype(F32)
    count = 2.0 * lax.psum(live_pairs[0].astype(F32), "rows")
    factor = 0.2 * N * scale / count
    signed = masks * 2 - 1
    bias = bias_in
    share = weights_in.shape[1]
    whole = lax.all_gather(weights_in, "rows", axis=1, tiled=True)
    for iteration in range(ITERS + 1):
        part = lax.dot_general(
            signed, whole.astype(BF16), (((1,), (1,)), ((), ())), preferred_element_type=F32
        )
        total = lax.psum(part, "cols") * scale
        upper = live * (total + bias - targets[0])
        lower = live * (-total + bias - targets[1])
        if iteration < ITERS:
            stacked = jnp.concatenate([upper.astype(BF16), lower.astype(BF16)], 1)
            both = lax.dot_general(
                stacked, signed, (((0,), (0,)), ((), ())), preferred_element_type=F32
            )
            k = upper.shape[1]
            raw, bias_sum = lax.psum((both[:k] - both[k:], jnp.sum(upper + lower, 0)), "rows")
            whole = shrink(whole - factor * raw, threshold[:, None])
            bias = bias - 0.5 * bias_sum / count
    weights = lax.dynamic_slice_in_dim(whole, lax.axis_index("rows") * share, share, 1)
    return weights, bias, jnp.stack([upper, lower], 0)


GROUPS = ((0, 24), (24, 16))
LEAD = 1
PER_GROUP = 22


def folded(size, tiles):
    return size // 16 * tiles * LANES + size % 16 // 8 * ((tiles + 1) // 2) * LANES


def body(
    tiles, nz,
    masks_hbm, targets_hbm, w_hbm, bias_in, thr, live_pairs,
    w_out, b_out, res_out,
    sm, wf, w_in, targets, mask_sem, w_sem, targets_sem, *per_group,
):
    k_rows, share = w_in.shape
    slots = sm.shape[0]
    win = tiles * LANES
    half = (tiles + 1) // 2 * LANES
    tail = win - half
    scale = 1.0 / math.sqrt(N)

    r = lax.axis_index("rows")
    c = lax.axis_index("cols")
    z = r // 2
    x = r % 2
    xpeer = z * 2 + (1 - x)

    def owner(k, other):
        zk = lax.rem(z + k, nz)
        return zk * 2 + ((1 - x) if other else x)

    def sender_to(k, other):
        zk = lax.rem(z + (nz - k), nz)
        return zk * 2 + ((1 - x) if other else x)

    def start_of(o):
        return pl.multiple_of((o * share) // LANES * LANES, LANES)

    offset = r * share - (r * share) // LANES * LANES

    w_copy = pltpu.make_async_copy(w_hbm, w_in, w_sem)
    w_copy.start()
    mask_copy = pltpu.make_async_copy(masks_hbm, sm, mask_sem)
    mask_copy.start()
    targets_copy = pltpu.make_async_copy(targets_hbm, targets, targets_sem)
    targets_copy.start()

    barrier = pltpu.get_barrier_semaphore()
    for k in range(nz):
        for other in (0, 1):
            if k or other:
                pl.semaphore_signal(
                    barrier, inc=1, device_id={"rows": owner(k, other)},
                    device_id_type=pl.DeviceIdType.MESH,
                )
    pl.semaphore_signal(
        barrier, inc=1, device_id={"cols": 1 - c}, device_id_type=pl.DeviceIdType.MESH
    )

    pending = []

    def send(src, dst, ssem, rsem, where):
        copy = pltpu.make_async_remote_copy(
            src_ref=src, dst_ref=dst, send_sem=ssem, recv_sem=rsem,
            device_id=where, device_id_type=pl.DeviceIdType.MESH,
        )
        copy.start()
        pending.append(copy)
        return copy

    def recv(dst, rsem):
        pltpu.make_async_copy(dst, dst, rsem).wait()

    def pack(value, ref):
        at = 0
        for top in range(0, value.shape[0] // 16 * 16, 16):
            ref[:, at : at + win] = value[top : top + 16].astype(BF16)
            at += win
        if value.shape[0] % 16:
            last = value[-8:]
            ref[:, at : at + half] = jnp.concatenate(
                [last[:, :half], last[:, win - half :]], 0
            ).astype(BF16)

    def unpack(ref, size):
        parts = []
        at = 0
        for top in range(0, size // 16 * 16, 16):
            parts.append(ref[:, at : at + win].astype(F32))
            at += win
        if size % 16:
            both = ref[:, at : at + half].astype(F32)
            parts.append(jnp.concatenate([both[:8], both[8:, half - tail :]], 1))
        return jnp.concatenate(parts, 0) if len(parts) > 1 else parts[0]

    lane = lax.broadcasted_iota(jnp.int32, (1, win), 1)
    mine = (lane >= offset) & (lane < offset + share)
    w_copy.wait()
    wf[:, 0:share] = w_in[...]
    wf[:, share:win] = jnp.zeros((k_rows, win - share), F32)
    wf[...] = pltpu.roll(wf[...], offset, 1)

    def send_own(g, t):
        (ag, *_, own_send, _, z_recv, x_recv) = per_group[g * PER_GROUP : g * PER_GROUP + 13]
        top, size = GROUPS[g]
        own = ag.at[t, 0, 0]
        pack(wf[top : top + size], own)
        for k in range(1, nz):
            send(own, ag.at[t, k, 0], own_send.at[t, k], z_recv.at[t, k], {"rows": sender_to(k, 0)})
        send(own, ag.at[t, 0, 1], own_send.at[t, 0], x_recv.at[t, 0], {"rows": xpeer})

    live = (lax.broadcasted_iota(jnp.int32, (1, slots), 1) < live_pairs[0]).astype(F32)
    last_lane = lax.broadcasted_iota(jnp.int32, (1, LANES), 1) == LANES - 1

    def chain(g):
        (
            ag, xs, xr, zs, zr, bs, br, ss, sr,
            own_send, fwd_send, z_recv, x_recv,
            xs_send, xs_recv, zs_send, zs_recv, b_send, b_recv, s_send, s_recv, counted,
        ) = per_group[g * PER_GROUP : (g + 1) * PER_GROUP]
        top, size = GROUPS[g]
        mid = slice(top, top + size)
        pick = (
            lax.broadcasted_iota(jnp.int32, (size, k_rows), 0) + top
            == lax.broadcasted_iota(jnp.int32, (size, k_rows), 1)
        ).astype(F32)
        eye = (
            lax.broadcasted_iota(jnp.int32, (size, LANES), 0)
            == lax.broadcasted_iota(jnp.int32, (size, LANES), 1)
        ).astype(F32)
        bias = jnp.sum(pick * bias_in[...], 1, keepdims=True)
        bound = jnp.sum(pick * thr[...], 1, keepdims=True)

        def window_scores(t, k, other):
            block = unpack(ag.at[t, k, other], size).astype(BF16)
            start = start_of(owner(k, other))
            return lax.dot_general(
                block, sm[:, pl.ds(start, win)], (((1,), (1,)), ((), ())),
                preferred_element_type=F32,
            )

        def gradient(stacked, k, other):
            start = start_of(owner(k, other))
            both = jnp.dot(stacked, sm[:, pl.ds(start, win)], preferred_element_type=F32)
            return both[:size] - both[size:]

        for t in range(ITERS + 1):
            part = window_scores(t, 0, 0)
            for k in range(1, nz):
                recv(ag.at[t, k, 0], z_recv.at[t, k])
                send(
                    ag.at[t, k, 0], ag.at[t, k, 1], fwd_send.at[t, k], x_recv.at[t, k],
                    {"rows": xpeer},
                )
                part += window_scores(t, k, 0)
            yield
            for k in range(nz):
                recv(ag.at[t, k, 1], x_recv.at[t, k])
                part += window_scores(t, k, 1)
            ss[t] = part
            copy = send(ss.at[t], sr.at[t], s_send.at[t], s_recv.at[t], {"cols": 1 - c})
            yield
            copy.wait_recv()
            total = (ss[t] + sr[t]) * scale
            upper = live * (total + bias - targets[0, mid])
            lower = live * (-total + bias - targets[1, mid])
            if t == ITERS:
                res_out[0, mid] = upper
                res_out[1, mid] = lower
                counted[...] = jnp.broadcast_to(jnp.sum(pick * bias, 0, keepdims=True), counted.shape)
                return

            stacked = jnp.concatenate([upper, lower], 0).astype(BF16)
            for k in list(range(1, nz)) + [0]:
                pack(gradient(stacked, k, 1), xs.at[t, k])
                send(xs.at[t, k], xr.at[t, k], xs_send.at[t, k], xs_recv.at[t, k], {"rows": xpeer})

            column = jnp.sum(upper + lower, 1, keepdims=True)
            row = jnp.sum(column * eye, 0, keepdims=True)
            row = jnp.where(last_lane, live_pairs[0].astype(F32), row)
            bs[t] = jnp.broadcast_to(row, (8, LANES))
            br[t, r] = jnp.broadcast_to(row, (8, LANES))
            for k in range(nz):
                for other in (0, 1):
                    if k or other:
                        send(
                            bs.at[t], br.at[t, r], b_send.at[t, k, other], b_recv.at[t, k, other],
                            {"rows": sender_to(k, other)},
                        )
            yield

            for k in range(1, nz):
                own = gradient(stacked, k, 0)
                recv(xr.at[t, k], xs_recv.at[t, k])
                pack(own + unpack(xr.at[t, k], size), zs.at[t, k])
                send(
                    zs.at[t, k], zr.at[t, k], zs_send.at[t, k], zs_recv.at[t, k],
                    {"rows": owner(k, 0)},
                )
            yield

            raw = gradient(stacked, 0, 0)
            recv(xr.at[t, 0], xs_recv.at[t, 0])
            raw += unpack(xr.at[t, 0], size)
            for k in range(nz):
                for other in (0, 1):
                    if k or other:
                        recv(br.at[t, owner(k, other)], b_recv.at[t, k, other])
            sums = br[t, 0]
            for j in range(1, 2 * nz):
                sums += br[t, j]
            sums = sums[0:1]
            count = 2.0 * jnp.sum(jnp.where(last_lane, sums, 0.0), 1, keepdims=True)
            bias_sum = jnp.sum(sums * eye, 1, keepdims=True)
            factor = 0.2 * N * scale / count
            bias = bias - 0.5 * bias_sum / count
            for k in range(1, nz):
                recv(zr.at[t, k], zs_recv.at[t, k])
                raw += unpack(zr.at[t, k], size)
            wf[mid] = jnp.where(mine, shrink(wf[mid] - factor * raw, bound), 0.0)
            send_own(g, t + 1)
            yield

    pl.semaphore_wait(barrier, 2 * nz)
    for g in range(len(GROUPS)):
        send_own(g, 0)
    mask_copy.wait()
    targets_copy.wait()
    for i in range(slots // 16):
        rows = pl.ds(i * 16, 16)
        sm[rows, :] = sm[rows, :] * 2 - 1

    chains = [chain(g) for g in range(len(GROUPS))]
    for ahead in range(LEAD):
        next(chains[0], None)
    turn = 1
    alive = set(range(len(chains)))
    while alive:
        g = turn % len(chains)
        turn += 1
        if g in alive:
            try:
                next(chains[g])
            except StopIteration:
                alive.remove(g)

    final = sum(per_group[g * PER_GROUP + PER_GROUP - 1][0:1] for g in range(len(GROUPS)))
    b_out[...] = final
    w_out[...] = pltpu.roll(wf[...], lax.rem(win - offset, win), 1)[:, :share]
    for copy in pending:
        copy.wait_send()


def fused(rows, masks, targets, weights_in, bias_in, threshold, live_pairs):
    slots, cols = masks.shape
    k_rows, share = weights_in.shape
    nz = rows // 2
    tiles = max(-(-share * (j + 1) // LANES) - share * j // LANES for j in range(rows))
    turns = ITERS + 1
    dma = pltpu.SemaphoreType.DMA
    vmem = pl.BlockSpec(memory_space=pltpu.VMEM)
    hbm = pl.BlockSpec(memory_space=pltpu.HBM)
    per_group = []
    for top, size in GROUPS:
        packed = (16, folded(size, tiles))
        mine = [
            pltpu.VMEM((turns, nz, 2) + packed, BF16),
            pltpu.VMEM((ITERS, nz) + packed, BF16),
            pltpu.VMEM((ITERS, nz) + packed, BF16),
            pltpu.VMEM((ITERS, nz) + packed, BF16),
            pltpu.VMEM((ITERS, nz) + packed, BF16),
            pltpu.VMEM((ITERS, 8, LANES), F32),
            pltpu.VMEM((ITERS, rows, 8, LANES), F32),
            pltpu.VMEM((turns, size, slots), F32),
            pltpu.VMEM((turns, size, slots), F32),
            dma((turns, nz)), dma((turns, nz)), dma((turns, nz)), dma((turns, nz)),
            dma((ITERS, nz)), dma((ITERS, nz)), dma((ITERS, nz)), dma((ITERS, nz)),
            dma((ITERS, nz, 2)), dma((ITERS, nz, 2)),
            dma((turns,)), dma((turns,)),
            pltpu.VMEM((8, k_rows), F32),
        ]
        per_group += mine
    weights, bias, residual = pl.pallas_call(
        functools.partial(body, tiles, nz),
        out_shape=(
            jax.ShapeDtypeStruct((k_rows, share), F32),
            jax.ShapeDtypeStruct((1, k_rows), F32),
            jax.ShapeDtypeStruct((2, k_rows, slots), F32),
        ),
        in_specs=[
            hbm, hbm, hbm, vmem, vmem,
            pl.BlockSpec(memory_space=pltpu.SMEM),
        ],
        out_specs=(vmem, vmem, vmem),
        scratch_shapes=[
            pltpu.VMEM((slots, cols), BF16),
            pltpu.VMEM((k_rows, tiles * LANES), F32),
            pltpu.VMEM((k_rows, share), F32),
            pltpu.VMEM((2, k_rows, slots), F32),
            dma, dma, dma,
        ] + per_group,
        compiler_params=pltpu.CompilerParams(
            collective_id=0, has_side_effects=True, vmem_limit_bytes=48 * 1024 * 1024
        ),
    )(
        masks, jnp.swapaxes(targets, 1, 2), weights_in,
        bias_in[None], threshold[None], live_pairs,
    )
    return weights, bias[0], jnp.swapaxes(residual, 1, 2)


def solution(mesh):
    rows = mesh.shape["rows"]
    on_device = functools.partial(fused, rows) if rows == 8 else plain
    return jax.shard_map(
        on_device,
        mesh=mesh,
        in_specs=(
            P(("grp", "rows"), "cols"),
            P(None, ("grp", "rows"), None),
            P("grp", ("cols", "rows")),
            P("grp"),
            P("grp"),
            P(("grp", "rows")),
        ),
        out_specs=(P("grp", ("cols", "rows")), P("grp"), P(None, ("grp", "rows"), None)),
        check_vma=False,
    )
```

time: 114 us -> 102 us (0.89)
  Pallas kernels: 105 us -> 93.2 us
    pallas_call x1, Pallas kernels: 105 us -> 93.2 us  [fused(): pl.pallas_call(functools.partial(body, tiles, nz), out_shape=(jax.ShapeDt...]
    unnamed x8 -> x13, local copies, waits for them, and re-layouts: 5.31 us -> 7.13 us
    broadcast_in_dim x2 -> x0, local copies, waits for them, and re-layouts: 1.48 us -> none  [the longest x1 0.74 us: fused(): bias_in[:, None]]
where the time goes in v2:
time: 102 us
  Pallas kernels  93.2 us (91%)
  local copies, waits for them, and re-layouts  7.13 us (7%)
  between operations  1.3 us (1%)
    pallas_call x1, Pallas kernels, fused(): pl.pallas_call(functools.partial(body, tiles, nz), out_shape=(jax.ShapeDt...  93.2 us
    unnamed x13, local copies, waits for them, and re-layouts  7.13 us

profile of v2, /device:TPU:1, one launch (start us, length us, event | category | flops | bytes accessed | tf_op | source)
XLA Modules:
  0.0 101.7 jit_solution(18079075696100566346)
XLA Ops:
  1.3 0.0 copy-start
  1.3 2.1 %copy-done = bf16[160,12544]{1,0:T(8,128)(2,1)S(1)} copy-done((bf16[160,12544]{1,0:T(8,128)(2,1)S(1)}, bf16[160,12544]{1,0:T(8,128)(2,1)}, u32[]{:S(2)}) %copy-start) | copy-done | bytes 4014104
  3.4 0.0 copy-start.1
  3.4 0.9 copy-done.1
  4.4 0.0 copy-start.2
  4.4 0.9 copy-done.2
  5.3 0.0 copy-start.3
  5.3 0.7 copy-done.3
  5.9 0.0 copy-start.4
  5.9 0.7 copy-done.4
  6.6 93.2 %shard_map.85 = (f32[40,1568]{1,0:T(8,128)S(1)}, f32[1,40]{1,0:T(1,128)S(1)}, f32[2,40,160]{2,1,0:T(8,128)S(1)}) custom-call(bf16[160,12544]{1,0:T(8,128)(2,1)S(1)} %copy-done, f32[2,40,160]{2,1,0:T(8,128)S(1)} %bitcast.6, f32[40,1568]{1,0:T(8,128)S(1)} %copy-done.1, f32[1,40]{1,0:T(1,128)S(1)} %bitcast.7, f32[1,40]{1,0:T(1,128)S(1)} %bitcast.8, ...), custom_call_target="tpu_custom_call" | custom-call | tf_op jit(solution)/shard_map/pallas_call | solution.py:335
  99.8 0.7 copy.13
  100.5 0.5 copy.14
  101.0 0.6 copy.15
Async XLA Ops:
  1.3 2.1 %copy-start = (bf16[160,12544]{1,0:T(8,128)(2,1)S(1)}, bf16[160,12544]{1,0:T(8,128)(2,1)}, u32[]{:S(2)}) copy-start(bf16[160,12544]{1,0:T(8,128)(2,1)} %masks_hbm.1) | copy-start | bytes 12042244
  3.4 1.0 copy-start.1
  4.4 0.9 copy-start.2
  5.3 0.7 copy-start.3
  5.9 0.7 copy-start.4
